TPU v7x, 32 devices: a whole 2x2x4 slice. The times are simulated.
32 devices in a mesh: seq: 8 (over z, y), head: 4 (over x, core).
Axes of the slice: x: 2, y: 2, z: 4, core: 2. Of those that a mesh axis runs over, the one named last changes fastest.
Arguments:
- qkv: bfloat16 [2, 3, 1024, 8, 128], P(None, None, 'seq', 'head'), may hold values from -48 to 48
- out_weight: bfloat16 [2, 8, 128, 2048], P(None, 'head'), may hold values from -0.59765625 to 0.59765625
- out_grad: bfloat16 [1024, 2048], P('seq', 'head'), may hold values from -6 to 6
Outputs:
- mixed: bfloat16 [1024, 2048], P('seq', 'head')
- grads: bfloat16 [2, 3, 1024, 8, 128], P(None, None, 'seq', 'head')
All inputs are finite; a program needn't handle non-finite values.
Results may differ from a plain program's by a relative error of at most 0.039.
Values may be sent and summed in bfloat16 or wider, within the bound.
A program may use at most 64 MiB of HBM per device.

v0:
```python
import functools
import math

import jax
import jax.numpy as jnp
from jax import lax
from jax.experimental import pallas as pl
from jax.experimental.pallas import tpu as pltpu
from jax.sharding import PartitionSpec as P

ROW = 512
MESH = pl.DeviceIdType.MESH
F32 = jnp.float32
BF16 = jnp.bfloat16


def dot_nn(a, b):
    return lax.dot_general(a, b, (((1,), (0,)), ((), ())), preferred_element_type=F32)


def dot_nt(a, b):
    return lax.dot_general(a, b, (((1,), (1,)), ((), ())), preferred_element_type=F32)


def dot_tn(a, b):
    return lax.dot_general(a, b, (((0,), (0,)), ((), ())), preferred_element_type=F32)


def layer_kernel(
    seq_count, head_groups, back, lines,
    qkv_hbm, w_hbm, og_hbm, mixed, grads,
    w, qkv, og, kvw, skv, ogf, even, odd, mate_in, up_out, up_in, sdks, sdkr, mxs, mxr, dos, att,
    in_sem, ss, rs,
):
    r = lax.axis_index("seq")
    me = lax.axis_index("head")
    heads, shard, width = qkv.shape[2:]
    cols = og.shape[1]
    scale = 1.0 / math.sqrt(width)
    side = lax.rem(r, 2)
    mate = r + 1 - 2 * side
    far = list(range(1, lines))
    steps = list(range(2, back + 1, 2))

    own_copy = pltpu.make_async_copy(
        qkv_hbm.at[0, 1:3], kvw.at[:, :, pl.ds(0, shard)], in_sem.at[0]
    )
    qkv_copy = pltpu.make_async_copy(qkv_hbm, qkv, in_sem.at[1])
    og_load = pltpu.make_async_copy(og_hbm, og, in_sem.at[2])
    w_copy = pltpu.make_async_copy(w_hbm, w, in_sem.at[3])
    for copy in (own_copy, og_load, qkv_copy, w_copy):
        copy.start()

    spans = sorted({2} | {back * j for j in far})
    barrier = pltpu.get_barrier_semaphore()
    expected = jnp.int32(head_groups)
    pl.semaphore_signal(barrier, inc=1, device_id={"seq": mate}, device_id_type=MESH)
    for k in range(1, head_groups):
        pl.semaphore_signal(
            barrier, inc=1, device_id={"head": lax.rem(me + k, head_groups)}, device_id_type=MESH
        )
    for d in spans:
        for target in (r + d, r - d):
            there = (target >= 0) & (target < seq_count)
            expected = expected + jnp.where(there, 1, 0)

            @pl.when(there)
            def _(target=target):
                pl.semaphore_signal(barrier, inc=1, device_id={"seq": target}, device_id_type=MESH)

    def after(d):
        return r + d < seq_count

    def before(d):
        return r - d >= 0

    def absent(there, ref):
        @pl.when(jnp.logical_not(there))
        def _():
            ref[...] = jnp.zeros(ref.shape, ref.dtype)

    def mate_sends(e):
        return before(e) & ((side == 1) if e == back else (side == 0) if e == 0 else True)

    def slot(d):
        return pl.ds(d * shard, shard)

    for d in range(1, back + 1):
        absent(before(d), kvw.at[:, :, slot(d)])
    for j in far:
        absent(before(back * j), skv.at[j - 1])
        absent(after(back * j), sdkr.at[j - 1])
    for e in [0] + steps:
        absent(mate_sends(e), mate_in.at[e // 2])
        if e < back:
            absent(after(2) & before(e), up_in.at[e // 2])

    base = [0]

    def numbered(count):
        first = base[0]
        base[0] += count
        return first

    og_at, mx_at = numbered(head_groups), numbered(head_groups)
    skv_at, sdk_at = numbered(lines), numbered(lines)
    kv_at, odd_at = numbered((back + 1) * heads), numbered((back + 1) * heads)
    up_at = numbered((back + 1) * heads)

    def remote(source, target, send_at, recv_at, device):
        return pltpu.make_async_remote_copy(
            src_ref=source, dst_ref=target, send_sem=ss.at[send_at], recv_sem=rs.at[recv_at],
            device_id=device, device_id_type=MESH,
        )

    def og_copy(k):
        device = {"head": lax.rem(me + k, head_groups)}
        return remote(og, ogf.at[k - 1], og_at + k, og_at + k, device)

    def mx_copy(k):
        device = {"head": lax.rem(me + k, head_groups)}
        return remote(mxs.at[k - 1], mxr.at[k - 1], mx_at + k, mx_at + k, device)

    def skv_copy(j):
        at = skv_at + j
        return remote(qkv.at[1, 1:3], skv.at[j - 1], at, at, {"seq": r + back * j})

    def sdk_copy(j):
        at = sdk_at + j
        return remote(sdks.at[j - 1], sdkr.at[j - 1], at, at, {"seq": r - back * j})

    def down_copy(d, h):
        at = kv_at + d * heads + h
        return remote(kvw.at[:, h, slot(d - 2)], kvw.at[:, h, slot(d)], at, at, {"seq": r + 2})

    def cross_copy(d, h):
        at = kv_at + d * heads + h
        source = pl.ds(pl.multiple_of((d - 1 + 2 * side) * shard, shard), shard)
        return remote(kvw.at[:, h, source], kvw.at[:, h, slot(d)], at, at, {"seq": mate})

    def pass_on(e, h):
        if e < back:
            pl.when(after(2) & before(e))(lambda: down_copy(e + 2, h).start())
            pl.when((side == 0) & before(e))(lambda: cross_copy(e + 1, h).start())
        if e > 0:
            pl.when((side == 1) & before(e))(lambda: cross_copy(e - 1, h).start())

    def odd_copy(d, h):
        into = (d + 1 - 2 * side) // 2
        at = odd_at + into * heads + h
        return remote(odd.at[d // 2, :, h], mate_in.at[into, :, h], odd_at + d * heads + h, at, {"seq": mate})

    def mate_wait(e, h):
        at = odd_at + (e // 2) * heads + h
        copy = remote(odd.at[0, :, h], mate_in.at[e // 2, :, h], at, at, {"seq": mate})
        pl.when(mate_sends(e))(lambda: copy.wait_recv())

    def up_copy(e, h):
        at = up_at + e * heads + h
        return remote(up_out.at[e // 2 - 1, :, h], up_in.at[e // 2 - 1, :, h], at, at, {"seq": r - 2})

    def gathered(e, h):
        mate_wait(e, h)
        total = even[e // 2, :, h] + mate_in[e // 2, :, h].astype(F32)
        if e < back:
            pl.when(after(2) & before(e))(lambda: up_copy(e + 2, h).wait_recv())
            total = total + up_in[e // 2, :, h].astype(F32)
        return total

    def send_up(e, h):
        up_out[e // 2 - 1, :, h] = gathered(e, h).astype(BF16)
        pl.when(before(e))(lambda: up_copy(e, h).start())

    own_copy.wait()
    pl.semaphore_wait(barrier, expected)
    for h in range(heads):
        pass_on(0, h)
    og_load.wait()
    for k in range(1, head_groups):
        og_copy(k).start()
    qkv_copy.wait()
    w_copy.wait()

    def w_cols(group):
        return w[:, pl.ds(pl.multiple_of(group * cols, cols), cols)]

    total = dot_nt(og[...], w_cols(me))
    for e in steps:
        for h in range(heads):
            pl.when(before(e))(lambda e=e, h=h: down_copy(e, h).wait_recv())
            pass_on(e, h)
    for j in far:
        pl.when(after(back * j))(lambda j=j: skv_copy(j).start())

    for k in range(1, head_groups):
        og_copy(k).wait_recv()
        total += dot_nt(ogf[k - 1], w_cols(lax.rem(me + head_groups - k, head_groups)))
    dos[...] = total.astype(BF16)

    window = (back + 1) * shard
    row = lax.broadcasted_iota(jnp.int32, (shard, window), 0)
    col = lax.broadcasted_iota(jnp.int32, (shard, window), 1)
    near = col // shard
    apart = near * shard + row - (col - near * shard)
    allowed = (apart >= 0) & (apart < ROW) & (near <= r)
    for h in range(heads):
        for d in range(1, back, 2):
            pl.when(before(d))(lambda d=d, h=h: cross_copy(d, h).wait_recv())
        q, keys, values = qkv[0, 0, h], kvw[0, h], kvw[1, h]
        do = dos[:, h * width:(h + 1) * width]
        scores = jnp.where(allowed, dot_nt(q, keys) * scale, -jnp.inf)
        raised = jnp.exp(scores - jnp.max(scores, axis=1, keepdims=True))
        probs = raised / jnp.sum(raised, axis=1, keepdims=True)
        weights = probs.astype(BF16)
        out = dot_nn(weights, values).astype(BF16)
        att[:, h * width:(h + 1) * width] = out
        delta = jnp.sum(do.astype(F32) * out.astype(F32), axis=1, keepdims=True)
        grad_s = (probs * (dot_nt(do, values) - delta)).astype(BF16)
        pair = (dot_tn(grad_s, q) * scale, dot_tn(weights, do))
        for i in range(2):
            for d in range(back + 1):
                part = pair[i][d * shard:(d + 1) * shard]
                if d % 2:
                    odd[d // 2, i, h] = part.astype(BF16)
                else:
                    even[d // 2, i, h] = part
        for d in reversed(range(1, back, 2)):
            pl.when(before(d))(lambda d=d, h=h: odd_copy(d, h).start())
        grads[0, 0, h] = (dot_nn(grad_s, keys) * scale).astype(BF16)
    for h in range(heads):
        send_up(back, h)

    for j in far:
        pl.when(before(back * j))(lambda j=j: skv_copy(j).wait_recv())

    def key_of(j, h):
        return (qkv[1, 1, h] if j == 0 else skv[j - 1, 0, h]).astype(F32)

    def value_of(j, h):
        return (qkv[1, 2, h] if j == 0 else skv[j - 1, 1, h]).astype(F32)

    strided_probs = []
    for h in range(heads):
        q = qkv[1, 0, h].astype(F32)
        scores = [jnp.sum(q * key_of(0, h), axis=1, keepdims=True) * scale]
        for j in far:
            score = jnp.sum(q * key_of(j, h), axis=1, keepdims=True) * scale
            scores.append(jnp.where(before(back * j), score, -jnp.inf))
        largest = functools.reduce(jnp.maximum, scores)
        raised = [jnp.exp(s - largest) for s in scores]
        sums = sum(raised)
        probs = [e / sums for e in raised]
        strided_probs.append(probs)
        out = sum(p.astype(BF16).astype(F32) * value_of(j, h) for j, p in enumerate(probs))
        att[:, (heads + h) * width:(heads + h + 1) * width] = out.astype(BF16)

    for k in range(1, head_groups):
        mxs[k - 1] = dot_nn(att[...], w_cols(lax.rem(me + k, head_groups))).astype(BF16)
        mx_copy(k).start()

    for e in reversed(steps[:-1]):
        for h in range(heads):
            send_up(e, h)

    strided_own = []
    for h in range(heads):
        lanes = slice((heads + h) * width, (heads + h + 1) * width)
        q, do = qkv[1, 0, h].astype(F32), dos[:, lanes].astype(F32)
        delta = jnp.sum(do * att[:, lanes].astype(F32), axis=1, keepdims=True)
        grad_q = jnp.zeros_like(q)
        for j in [0] + far:
            prob = strided_probs[h][j]
            grad_p = jnp.sum(do * value_of(j, h), axis=1, keepdims=True)
            grad_s = (prob * (grad_p - delta)).astype(BF16).astype(F32)
            grad_q += grad_s * key_of(j, h)
            grad_k = grad_s * q * scale
            grad_v = prob.astype(BF16).astype(F32) * do
            if j == 0:
                strided_own.append((grad_k, grad_v))
            else:
                sdks[j - 1, 0, h] = grad_k.astype(BF16)
                sdks[j - 1, 1, h] = grad_v.astype(BF16)
        grads[1, 0, h] = (grad_q * scale).astype(BF16)
    for j in far:
        pl.when(before(back * j))(lambda j=j: sdk_copy(j).start())

    total = dot_nn(att[...], w_cols(me))
    for h in range(heads):
        grads[0, 1:3, h] = gathered(0, h).astype(BF16)
    for k in range(1, head_groups):
        mx_copy(k).wait_recv()
        total += mxr[k - 1].astype(F32)
    mixed[...] = total.astype(BF16)
    for j in far:
        pl.when(after(back * j))(lambda j=j: sdk_copy(j).wait_recv())
    for h in range(heads):
        for i in range(2):
            grads[1, 1 + i, h] = (
                strided_own[h][i] + sum(sdkr[j - 1, i, h].astype(F32) for j in far)
            ).astype(BF16)

    for k in range(1, head_groups):
        og_copy(k).wait_send()
        mx_copy(k).wait_send()
    for h in range(heads):
        for e in [0] + steps:
            if e < back:
                pl.when(after(2) & before(e))(lambda e=e, h=h: down_copy(e + 2, h).wait_send())
            if e > 0:
                pl.when(before(e))(lambda e=e, h=h: up_copy(e, h).wait_send())
        for d in range(1, back, 2):
            pl.when(before(d - 1 + 2 * side))(lambda d=d, h=h: cross_copy(d, h).wait_send())
            pl.when(before(d))(lambda d=d, h=h: odd_copy(d, h).wait_send())
    for j in far:
        pl.when(after(back * j))(lambda j=j: skv_copy(j).wait_send())
        pl.when(before(back * j))(lambda j=j: sdk_copy(j).wait_send())


def shards(seq_count, head_groups, qkv, out_weight, out_grad):
    _, _, shard, heads, width = qkv.shape
    back = ROW // shard
    assert back * shard == ROW and back % 2 == 0 and seq_count % back == 0
    lines = seq_count // back
    others = max(1, lines - 1)
    model = out_weight.shape[-1]
    cols = out_grad.shape[1]
    pairs = (2, heads, shard, width)
    copies = 2 * (head_groups + lines) + 3 * (back + 1) * heads
    vmem = pl.BlockSpec(memory_space=pltpu.VMEM)
    hbm = pl.BlockSpec(memory_space=pl.ANY)
    mixed, grads = pl.pallas_call(
        functools.partial(layer_kernel, seq_count, head_groups, back, lines),
        out_shape=[
            jax.ShapeDtypeStruct((shard, cols), BF16),
            jax.ShapeDtypeStruct((2, 3, heads, shard, width), BF16),
        ],
        in_specs=[hbm, hbm, hbm],
        out_specs=[vmem, vmem],
        scratch_shapes=[
            pltpu.VMEM((2 * heads * width, model), BF16),
            pltpu.VMEM((2, 3, heads, shard, width), BF16),
            pltpu.VMEM((shard, cols), BF16),
            pltpu.VMEM((2, heads, (back + 1) * shard, width), BF16),
            pltpu.VMEM((others,) + pairs, BF16),
            pltpu.VMEM((head_groups, shard, cols), BF16),
            pltpu.VMEM((back // 2 + 1,) + pairs, F32),
            pltpu.VMEM((back // 2,) + pairs, BF16),
            pltpu.VMEM((back // 2 + 1,) + pairs, BF16),
            pltpu.VMEM((back // 2,) + pairs, BF16),
            pltpu.VMEM((back // 2,) + pairs, BF16),
            pltpu.VMEM((others,) + pairs, BF16),
            pltpu.VMEM((others,) + pairs, BF16),
            pltpu.VMEM((head_groups, shard, cols), BF16),
            pltpu.VMEM((head_groups, shard, cols), BF16),
            pltpu.VMEM((shard, 2 * heads * width), BF16),
            pltpu.VMEM((shard, 2 * heads * width), BF16),
            pltpu.SemaphoreType.DMA((4,)),
            pltpu.SemaphoreType.DMA((copies,)),
            pltpu.SemaphoreType.DMA((copies,)),
        ],
        compiler_params=pltpu.CompilerParams(
            collective_id=0, has_side_effects=True, vmem_limit_bytes=60 * 1024 * 1024
        ),
    )(
        jnp.swapaxes(qkv, 2, 3),
        out_weight.reshape(2 * heads * width, model),
        out_grad,
    )
    return mixed, jnp.swapaxes(grads, 2, 3)


def solution(mesh):
    return jax.shard_map(
        functools.partial(shards, mesh.shape["seq"], mesh.shape["head"]),
        mesh=mesh,
        in_specs=(
            P(None, None, "seq", "head", None),
            P(None, "head", None, None),
            P("seq", "head"),
        ),
        out_specs=(P("seq", "head"), P(None, None, "seq", "head", None)),
        check_vma=False,
    )
```

profile of v0, /device:TPU:0, one launch (start us, length us, event | category | flops | bytes accessed | tf_op | source)
XLA Modules:
  0.0 41.2 jit_solution(17051721487780493985)
XLA Ops:
  0.6 1.8 %copy.8 = bf16[2,3,128,2,128]{4,2,3,1,0:T(8,128)(2,1)} copy(bf16[2,3,128,2,128]{4,3,2,1,0:T(2,128)(2,1)} %param.3) | data formatting | bytes 786432 | tf_op args[0]
  2.4 35.0 %shard_map.50 = (bf16[128,512]{1,0:T(8,128)(2,1)}, bf16[2,3,2,128,128]{4,3,2,1,0:T(8,128)(2,1)}) custom-call(bf16[2,3,2,128,128]{4,3,2,1,0:T(8,128)(2,1)} %bitcast.6, bf16[512,2048]{1,0:T(8,128)(2,1)} %bitcast.5, bf16[128,512]{1,0:T(8,128)(2,1)} %og_hbm.1), custom_call_target="tpu_custom_call" | custom-call | tf_op jit(solution)/shard_map/pallas_call | solution.py:331
  37.5 2.1 %copy.6 = bf16[2,3,128,2,128]{4,3,2,1,0:T(2,128)(2,1)} copy(bf16[2,3,128,2,128]{4,2,3,1,0:T(8,128)(2,1)} %bitcast.7) | data formatting | bytes 786432
  39.6 1.6 %copy.10 = bf16[128,512]{1,0:T(8,128)(2,1)} copy(bf16[128,512]{1,0:T(8,128)(2,1)} %get-tuple-element.10) | data formatting | bytes 262144
where the time goes:
time: 41.4 us; the launch traced here: 41.2 us
  Pallas kernels  35 us (85%)
  local copies, waits for them, and re-layouts  5.52 us (13%)
  between operations  0.64 us (2%)
    pallas_call x1, Pallas kernels, shards(): pl.pallas_call(functools.partial(layer_kernel, seq_count, head_groups, ba...  35 us
    unnamed x3, local copies, waits for them, and re-layouts  5.52 us

commit v1 on v0

v1 whole, which is shorter than its diff:
```python
import functools
import math

import jax
import jax.numpy as jnp
from jax import lax
from jax.experimental import pallas as pl
from jax.experimental.pallas import tpu as pltpu
from jax.sharding import PartitionSpec as P

ROW = 512
MESH = pl.DeviceIdType.MESH
F32 = jnp.float32
BF16 = jnp.bfloat16


def dot_nn(a, b):
    return lax.dot_general(a, b, (((1,), (0,)), ((), ())), preferred_element_type=F32)


def dot_nt(a, b):
    return lax.dot_general(a, b, (((1,), (1,)), ((), ())), preferred_element_type=F32)


def layer_kernel(
    seq_count, head_groups, back, lines, spans,
    qkv_hbm, w_hbm, og_hbm, mixed, grads,
    w, qkv, og, kvw, qw, dow, skv, sqw, sdow, ogf, mxs, mxr, att, stats, in_sem, ss, rs,
):
    r = lax.axis_index("seq")
    me = lax.axis_index("head")
    heads, shard, width = qkv.shape[2:]
    cols = og.shape[1]
    scale = 1.0 / math.sqrt(width)
    side = lax.rem(r, 2)
    mate = r + 1 - 2 * side
    far = list(range(1, lines))
    steps = list(range(2, back + 1, 2))

    def slot(d):
        return pl.ds(d * shard, shard)

    loads = [
        pltpu.make_async_copy(source, target, in_sem.at[i])
        for i, (source, target) in enumerate([
            (qkv_hbm.at[0, 1:3], kvw.at[:, :, slot(0)]),
            (qkv_hbm.at[0, 0], qw.at[:, slot(0)]),
            (og_hbm, og),
            (qkv_hbm, qkv),
            (w_hbm, w),
        ])
    ]
    for load in loads:
        load.start()

    turn = 1 - 2 * lax.rem(me, 2)
    partners = []
    for m in range(2, head_groups, 2):
        to, source = lax.rem(me + m, head_groups), lax.rem(me + head_groups - m, head_groups)
        partners += [(to, source), (to + turn, source + turn)]
    partners.append((me + turn, me + turn))

    barrier = pltpu.get_barrier_semaphore()
    expected = jnp.int32(head_groups - 1)
    for d in spans:
        for target in (r + d, r - d):
            there = (target >= 0) & (target < seq_count)
            expected = expected + jnp.where(there, 1, 0)

            @pl.when(there)
            def _(target=target):
                pl.semaphore_signal(barrier, inc=1, device_id={"seq": target}, device_id_type=MESH)
    for to, _ in partners:
        pl.semaphore_signal(barrier, inc=1, device_id={"head": to}, device_id_type=MESH)

    def after(d):
        return r + d < seq_count

    def before(d):
        return r - d >= 0

    def absent(there, *refs):
        @pl.when(jnp.logical_not(there))
        def _():
            for ref in refs:
                ref[...] = jnp.zeros(ref.shape, ref.dtype)

    for d in range(1, back + 1):
        absent(before(d), kvw.at[:, :, slot(d)])
        absent(after(d), qw.at[:, slot(d)], dow.at[:, slot(d)])
    for j in far:
        absent(before(back * j), skv.at[j - 1])
        absent(after(back * j), sqw.at[j - 1], sdow.at[j - 1])
    for i, d in enumerate(spans):
        absent(after(d), stats.at[i + 1])

    base = [0]

    def numbered(count):
        first = base[0]
        base[0] += count
        return first

    def remote(source, target, at, device):
        return pltpu.make_async_remote_copy(
            src_ref=source, dst_ref=target, send_sem=ss.at[at], recv_sem=rs.at[at],
            device_id=device, device_id_type=MESH,
        )

    class Cascade:
        def __init__(self, way, part):
            self.way, self.part = way, part
            self.rank = r if way == 1 else seq_count - 1 - r
            self.side = side if way == 1 else 1 - side
            self.at = numbered((back + 1) * heads)

        def has(self, d):
            return self.rank - d >= 0

        def onward(self, d, h):
            return remote(
                self.part(h, slot(d - 2)), self.part(h, slot(d)), self.at + d * heads + h,
                {"seq": r + 2 * self.way},
            )

        def across(self, d, h):
            source = pl.ds(pl.multiple_of((d - 1 + 2 * self.side) * shard, shard), shard)
            return remote(
                self.part(h, source), self.part(h, slot(d)), self.at + d * heads + h, {"seq": mate}
            )

        def goes_on(self, e):
            return (self.rank + 2 < seq_count) & self.has(e)

        def pass_on(self, e):
            for h in range(heads):
                if e:
                    pl.when(self.has(e))(lambda: self.onward(e, h).wait_recv())
                if e < back:
                    pl.when(self.goes_on(e))(lambda: self.onward(e + 2, h).start())
                    pl.when((self.side == 0) & self.has(e))(lambda: self.across(e + 1, h).start())
                if e:
                    pl.when((self.side == 1) & self.has(e))(lambda: self.across(e - 1, h).start())

        def finish(self, h):
            for d in range(1, back, 2):
                pl.when(self.has(d))(lambda: self.across(d, h).wait_recv())

        def sent(self):
            for h in range(heads):
                for e in [0] + steps[:-1]:
                    pl.when(self.goes_on(e))(lambda: self.onward(e + 2, h).wait_send())
                for d in range(1, back, 2):
                    pl.when(self.has(d - 1 + 2 * self.side))(lambda: self.across(d, h).wait_send())

    kv = Cascade(1, lambda h, rows: kvw.at[:, h, rows])
    query = Cascade(-1, lambda h, rows: qw.at[h, rows])
    cotangent = Cascade(-1, lambda h, rows: dow.at[h, rows])
    og_at, mx_at = numbered(head_groups), numbered(head_groups)
    skv_at, sq_at, sdo_at = numbered(lines), numbered(lines), numbered(lines)
    stat_at = numbered(len(spans))

    def og_copy(i):
        return remote(og, ogf.at[i], og_at + i, {"head": partners[i][0]})

    def mx_copy(i):
        return remote(mxs.at[i], mxr.at[i], mx_at + i, {"head": partners[i][0]})

    def skv_copy(j):
        return remote(qkv.at[1, 1:3], skv.at[j - 1], skv_at + j, {"seq": r + back * j})

    def sq_copy(j):
        return remote(qkv.at[1, 0], sqw.at[j - 1], sq_at + j, {"seq": r - back * j})

    def sdo_copy(j):
        return remote(sdow.at[lines - 1], sdow.at[j - 1], sdo_at + j, {"seq": r - back * j})

    def stat_copy(i):
        return remote(stats.at[0], stats.at[i + 1], stat_at + i, {"seq": r - spans[i]})

    for load in loads[:3]:
        load.wait()
    pl.semaphore_wait(barrier, expected)
    kv.pass_on(0)
    for i in range(len(partners)):
        og_copy(i).start()
    query.pass_on(0)
    for load in loads[3:]:
        load.wait()

    def w_cols(group):
        return w[:, pl.ds(pl.multiple_of(group * cols, cols), cols)]

    total = dot_nt(og[...], w_cols(me))
    for e in steps:
        kv.pass_on(e)
        query.pass_on(e)
    for j in far:
        pl.when(after(back * j))(lambda j=j: skv_copy(j).start())
        pl.when(before(back * j))(lambda j=j: sq_copy(j).start())

    for i in reversed(range(len(partners))):
        og_copy(i).wait_recv()
        total += dot_nt(ogf[i], w_cols(partners[i][1]))
    total = total.astype(BF16)
    for h in range(heads):
        dow[h, slot(0)] = total[:, h * width:(h + 1) * width]
        sdow[lines - 1, h] = total[:, (heads + h) * width:(heads + h + 1) * width]
    cotangent.pass_on(0)
    for j in far:
        pl.when(before(back * j))(lambda j=j: sdo_copy(j).start())

    window = (back + 1) * shard
    row = lax.broadcasted_iota(jnp.int32, (shard, window), 0)
    col = lax.broadcasted_iota(jnp.int32, (shard, window), 1)
    near = col // shard
    apart = near * shard + row - (col - near * shard)
    allowed = (apart >= 0) & (apart < ROW) & (near <= r)
    columns = [None] * (4 * heads)
    for h in range(heads):
        kv.finish(h)
        q, keys, values, do = qw[h, slot(0)], kvw[0, h], kvw[1, h], dow[h, slot(0)]
        scores = jnp.where(allowed, dot_nt(q, keys) * scale, -jnp.inf)
        largest = jnp.max(scores, axis=1, keepdims=True)
        raised = jnp.exp(scores - largest)
        sums = jnp.sum(raised, axis=1, keepdims=True)
        probs = raised / sums
        out = dot_nn(probs.astype(BF16), values).astype(BF16)
        att[:, h * width:(h + 1) * width] = out
        delta = jnp.sum(do.astype(F32) * out.astype(F32), axis=1, keepdims=True)
        columns[h], columns[heads + h] = largest + jnp.log(sums), delta
        grad_s = (probs * (dot_nt(do, values) - delta)).astype(BF16)
        grads[0, 0, h] = (dot_nn(grad_s, keys) * scale).astype(BF16)
        if h == 0:
            for e in steps[:-1]:
                cotangent.pass_on(e)

    for j in far:
        pl.when(before(back * j))(lambda j=j: skv_copy(j).wait_recv())

    def key_of(j, h):
        return (qkv[1, 1, h] if j == 0 else skv[j - 1, 0, h]).astype(F32)

    def value_of(j, h):
        return (qkv[1, 2, h] if j == 0 else skv[j - 1, 1, h]).astype(F32)

    strided_probs = []
    for h in range(heads):
        q, do = qkv[1, 0, h].astype(F32), sdow[lines - 1, h].astype(F32)
        scores = [jnp.sum(q * key_of(0, h), axis=1, keepdims=True) * scale]
        for j in far:
            score = jnp.sum(q * key_of(j, h), axis=1, keepdims=True) * scale
            scores.append(jnp.where(before(back * j), score, -jnp.inf))
        largest = functools.reduce(jnp.maximum, scores)
        raised = [jnp.exp(s - largest) for s in scores]
        sums = sum(raised)
        probs = [e / sums for e in raised]
        strided_probs.append(probs)
        out = sum(p.astype(BF16).astype(F32) * value_of(j, h) for j, p in enumerate(probs))
        out = out.astype(BF16)
        att[:, (heads + h) * width:(heads + h + 1) * width] = out
        columns[2 * heads + h] = largest + jnp.log(sums)
        columns[3 * heads + h] = jnp.sum(do * out.astype(F32), axis=1, keepdims=True)

    lane = lax.broadcasted_iota(jnp.int32, (shard, 128), 1)
    table = jnp.zeros((shard, 128), F32)
    for i, column in enumerate(columns):
        table = jnp.where(lane == i, column, table)
    stats[0] = table.T[:stats.shape[1]]
    for i, d in enumerate(spans):
        pl.when(before(d))(lambda i=i: stat_copy(i).start())

    for i, (to, _) in enumerate(partners):
        mxs[i] = dot_nn(att[...], w_cols(to)).astype(BF16)
        mx_copy(i).start()
    cotangent.pass_on(back)
    total = dot_nn(att[...], w_cols(me))

    strided = []
    for h in range(heads):
        q, do = qkv[1, 0, h].astype(F32), sdow[lines - 1, h].astype(F32)
        delta = columns[3 * heads + h]
        grad_q = jnp.zeros_like(q)
        for j in [0] + far:
            prob = strided_probs[h][j]
            grad_p = jnp.sum(do * value_of(j, h), axis=1, keepdims=True)
            grad_s = (prob * (grad_p - delta)).astype(BF16).astype(F32)
            grad_q += grad_s * key_of(j, h)
            if j == 0:
                strided.append((grad_s * q, prob.astype(BF16).astype(F32) * do))
        grads[1, 0, h] = (grad_q * scale).astype(BF16)

    for i, d in enumerate(spans):
        pl.when(after(d))(lambda i=i: stat_copy(i).wait_recv())
    apart = col - row
    allowed = (apart >= 0) & (apart < ROW) & (near < seq_count - r)
    later = [0] + [spans.index(d) + 1 for d in range(1, back + 1) if d in spans]
    later += [0] * (back + 1 - len(later))
    for h in range(heads):
        query.finish(h)
        cotangent.finish(h)
        queries, dos, key, value = qw[h], dow[h], kvw[0, h, slot(0)], kvw[1, h, slot(0)]
        lse = jnp.concatenate([stats[i, h:h + 1] for i in later], axis=1)
        delta = jnp.concatenate([stats[i, heads + h:heads + h + 1] for i in later], axis=1)
        probs = jnp.exp(jnp.where(allowed, dot_nt(key, queries) * scale - lse, -jnp.inf))
        grad_s = (probs * (dot_nt(value, dos) - delta)).astype(BF16)
        grads[0, 1, h] = (dot_nn(grad_s, queries) * scale).astype(BF16)
        grads[0, 2, h] = dot_nn(probs.astype(BF16), dos).astype(BF16)

    for j in far:
        @pl.when(after(back * j))
        def _(j=j):
            sq_copy(j).wait_recv()
            sdo_copy(j).wait_recv()
    for j in far:
        rows = stats[spans.index(back * j) + 1]
        table = jnp.concatenate([rows] * (128 // rows.shape[0]), axis=0).T
        for h in range(heads):
            q, do = sqw[j - 1, h].astype(F32), sdow[j - 1, h].astype(F32)
            lse = table[:, 2 * heads + h:2 * heads + h + 1]
            delta = table[:, 3 * heads + h:3 * heads + h + 1]
            score = jnp.sum(q * key_of(0, h), axis=1, keepdims=True) * scale
            prob = jnp.exp(jnp.where(after(back * j), score - lse, -jnp.inf))
            grad_p = jnp.sum(do * value_of(0, h), axis=1, keepdims=True)
            grad_s = (prob * (grad_p - delta)).astype(BF16).astype(F32)
            grad_k, grad_v = strided[h]
            strided[h] = (grad_k + grad_s * q, grad_v + prob.astype(BF16).astype(F32) * do)
    for h in range(heads):
        grads[1, 1, h] = (strided[h][0] * scale).astype(BF16)
        grads[1, 2, h] = strided[h][1].astype(BF16)

    for i in reversed(range(len(partners))):
        mx_copy(i).wait_recv()
        total += mxr[i].astype(F32)
    mixed[...] = total.astype(BF16)

    for i in range(len(partners)):
        og_copy(i).wait_send()
        mx_copy(i).wait_send()
    for cascade in (kv, query, cotangent):
        cascade.sent()
    for j in far:
        pl.when(after(back * j))(lambda j=j: skv_copy(j).wait_send())

        @pl.when(before(back * j))
        def _(j=j):
            sq_copy(j).wait_send()
            sdo_copy(j).wait_send()
    for i, d in enumerate(spans):
        pl.when(before(d))(lambda i=i: stat_copy(i).wait_send())


def shards(seq_count, head_groups, qkv, out_weight, out_grad):
    _, _, shard, heads, width = qkv.shape
    back = ROW // shard
    assert back * shard == ROW and back % 2 == 0 and seq_count % back == 0
    assert head_groups % 2 == 0
    lines = seq_count // back
    others = max(1, lines - 1)
    spans = [d for d in range(1, back + 1) if d < seq_count]
    spans += [back * j for j in range(2, lines)]
    model = out_weight.shape[-1]
    cols = out_grad.shape[1]
    window = (back + 1) * shard
    stat_rows = 4 * heads
    while 128 % stat_rows or stat_rows % 8:
        stat_rows += 1
    copies = 2 * head_groups + 3 * lines + 3 * (back + 1) * heads + len(spans)
    vmem = pl.BlockSpec(memory_space=pltpu.VMEM)
    hbm = pl.BlockSpec(memory_space=pltpu.HBM)
    mixed, grads = pl.pallas_call(
        functools.partial(layer_kernel, seq_count, head_groups, back, lines, spans),
        out_shape=[
            jax.ShapeDtypeStruct((shard, cols), BF16),
            jax.ShapeDtypeStruct((2, 3, heads, shard, width), BF16),
        ],
        in_specs=[pl.BlockSpec(memory_space=pl.ANY), hbm, hbm],
        out_specs=[vmem, vmem],
        scratch_shapes=[
            pltpu.VMEM((2 * heads * width, model), BF16),
            pltpu.VMEM((2, 3, heads, shard, width), BF16),
            pltpu.VMEM((shard, cols), BF16),
            pltpu.VMEM((2, heads, window, width), BF16),
            pltpu.VMEM((heads, window, width), BF16),
            pltpu.VMEM((heads, window, width), BF16),
            pltpu.VMEM((others, 2, heads, shard, width), BF16),
            pltpu.VMEM((others, heads, shard, width), BF16),
            pltpu.VMEM((lines, heads, shard, width), BF16),
            pltpu.VMEM((head_groups - 1, shard, cols), BF16),
            pltpu.VMEM((head_groups - 1, shard, cols), BF16),
            pltpu.VMEM((head_groups - 1, shard, cols), BF16),
            pltpu.VMEM((shard, 2 * heads * width), BF16),
            pltpu.VMEM((len(spans) + 1, stat_rows, shard), F32),
            pltpu.SemaphoreType.DMA((5,)),
            pltpu.SemaphoreType.DMA((copies,)),
            pltpu.SemaphoreType.DMA((copies,)),
        ],
        compiler_params=pltpu.CompilerParams(
            collective_id=0, has_side_effects=True, vmem_limit_bytes=40 * 1024 * 1024
        ),
    )(
        jnp.swapaxes(qkv, 2, 3),
        out_weight.reshape(2 * heads * width, model),
        out_grad,
    )
    return mixed, jnp.swapaxes(grads, 2, 3)


def solution(mesh):
    return jax.shard_map(
        functools.partial(shards, mesh.shape["seq"], mesh.shape["head"]),
        mesh=mesh,
        in_specs=(
            P(None, None, "seq", "head", None),
            P(None, "head", None, None),
            P("seq", "head"),
        ),
        out_specs=(P("seq", "head"), P(None, None, "seq", "head", None)),
        check_vma=False,
    )
```

time: 41.4 us -> 33.7 us (0.81)
  the two profiles are of different devices: /device:TPU:0 before, /device:TPU:1 now
where the time goes in v1:
time: 33.7 us; the launch traced here: 33.1 us
  Pallas kernels  27.1 us (80%)
  local copies, waits for them, and re-layouts  5.35 us (16%)
  between operations  0.65 us (2%)
    pallas_call x1, Pallas kernels, shards(): pl.pallas_call(functools.partial(layer_kernel, seq_count, head_groups, ba...  27.1 us
    unnamed x7, local copies, waits for them, and re-layouts  5.35 us

profile of v1, /device:TPU:1, one launch (start us, length us, event | category | flops | bytes accessed | tf_op | source)
XLA Modules:
  0.0 33.1 jit_solution(5229461917945028610)
XLA Ops:
  0.6 1.1 %copy.8 = bf16[2,3,128,2,128]{4,2,3,1,0:T(8,128)(2,1)S(1)} copy(bf16[2,3,128,2,128]{4,3,2,1,0:T(2,128)(2,1)} %param.3) | data formatting | bytes 786432 | tf_op args[0]
  1.7 0.0 copy-start
  1.7 1.6 %copy-done = bf16[2,2,128,2048]{3,2,1,0:T(8,128)(2,1)S(1)} copy-done((bf16[2,2,128,2048]{3,2,1,0:T(8,128)(2,1)S(1)}, bf16[2,2,128,2048]{3,2,1,0:T(8,128)(2,1)}, u32[]{:S(2)}) %copy-start) | copy-done | bytes 2097176
  3.3 0.0 copy-start.1
  3.3 0.9 %copy-done.1 = bf16[128,512]{1,0:T(8,128)(2,1)S(1)} copy-done((bf16[128,512]{1,0:T(8,128)(2,1)S(1)}, bf16[128,512]{1,0:T(8,128)(2,1)}, u32[]{:S(2)}) %copy-start.1) | copy-done | bytes 131096
  4.2 27.1 %shard_map.50 = (bf16[128,512]{1,0:T(8,128)(2,1)S(1)}, bf16[2,3,2,128,128]{4,3,2,1,0:T(8,128)(2,1)S(1)}) custom-call(bf16[2,3,2,128,128]{4,3,2,1,0:T(8,128)(2,1)S(1)} %bitcast.6, bf16[512,2048]{1,0:T(8,128)(2,1)S(1)} %bitcast.5, bf16[128,512]{1,0:T(8,128)(2,1)S(1)} %copy-done.1), custom_call_target="tpu_custom_call" | custom-call | tf_op jit(solution)/shard_map/pallas_call | solution.py:371
  31.3 1.2 %copy.6 = bf16[2,3,128,2,128]{4,3,2,1,0:T(2,128)(2,1)} copy(bf16[2,3,128,2,128]{4,2,3,1,0:T(8,128)(2,1)S(1)} %bitcast.7) | data formatting | bytes 786432
  32.4 0.7 %copy.10 = bf16[128,512]{1,0:T(8,128)(2,1)} copy(bf16[128,512]{1,0:T(8,128)(2,1)S(1)} %get-tuple-element.10) | data formatting | bytes 262144
Async XLA Ops:
  1.7 1.6 %copy-start = (bf16[2,2,128,2048]{3,2,1,0:T(8,128)(2,1)S(1)}, bf16[2,2,128,2048]{3,2,1,0:T(8,128)(2,1)}, u32[]{:S(2)}) copy-start(bf16[2,2,128,2048]{3,2,1,0:T(8,128)(2,1)} %param.4) | copy-start | bytes 6291460
  3.3 0.9 %copy-start.1 = (bf16[128,512]{1,0:T(8,128)(2,1)S(1)}, bf16[128,512]{1,0:T(8,128)(2,1)}, u32[]{:S(2)}) copy-start(bf16[128,512]{1,0:T(8,128)(2,1)} %og_hbm.1) | copy-start | bytes 393220

commit v2 on v1

--- a/solution.py
+++ b/solution.py
@@ -25,7 +25,7 @@
 def layer_kernel(
     seq_count, head_groups, back, lines, spans,
     qkv_hbm, w_hbm, og_hbm, mixed, grads,
-    w, qkv, og, kvw, qw, dow, skv, sqw, sdow, ogf, mxs, mxr, att, stats, in_sem, ss, rs,
+    w, qkv, og, kvw, qw, dow, skv, sqw, sdow, ogf, mxs, mxr, att, near_stats, far_stats, in_sem, ss, rs,
 ):
     r = lax.axis_index("seq")
     me = lax.axis_index("head")
@@ -87,12 +87,10 @@
 
     for d in range(1, back + 1):
         absent(before(d), kvw.at[:, :, slot(d)])
-        absent(after(d), qw.at[:, slot(d)], dow.at[:, slot(d)])
+        absent(after(d), qw.at[:, slot(d)], dow.at[:, slot(d)], near_stats.at[d])
     for j in far:
         absent(before(back * j), skv.at[j - 1])
-        absent(after(back * j), sqw.at[j - 1], sdow.at[j - 1])
-    for i, d in enumerate(spans):
-        absent(after(d), stats.at[i + 1])
+        absent(after(back * j), sqw.at[j - 1], sdow.at[j - 1], far_stats.at[j])
 
     base = [0]
 
@@ -158,7 +156,7 @@
     cotangent = Cascade(-1, lambda h, rows: dow.at[h, rows])
     og_at, mx_at = numbered(head_groups), numbered(head_groups)
     skv_at, sq_at, sdo_at = numbered(lines), numbered(lines), numbered(lines)
-    stat_at = numbered(len(spans))
+    near_at, far_at = numbered(back + 1), numbered(lines)
 
     def og_copy(i):
         return remote(og, ogf.at[i], og_at + i, {"head": partners[i][0]})
@@ -175,8 +173,21 @@
     def sdo_copy(j):
         return remote(sdow.at[lines - 1], sdow.at[j - 1], sdo_at + j, {"seq": r - back * j})
 
-    def stat_copy(i):
-        return remote(stats.at[0], stats.at[i + 1], stat_at + i, {"seq": r - spans[i]})
+    def near_copy(d):
+        return remote(near_stats.at[0], near_stats.at[d], near_at + d, {"seq": r - d})
+
+    def far_copy(j):
+        return remote(far_stats.at[0], far_stats.at[j], far_at + j, {"seq": r - back * j})
+
+    def as_rows(columns):
+        lane = lax.broadcasted_iota(jnp.int32, (shard, 128), 1)
+        table = jnp.zeros((shard, 128), F32)
+        for i, column in enumerate(columns):
+            table = jnp.where(lane == i, column, table)
+        return table.T[:near_stats.shape[1]]
+
+    def delta_of(do, out):
+        return jnp.sum(do.astype(F32) * out.astype(F32), axis=1, keepdims=True)
 
     for load in loads[:3]:
         load.wait()
@@ -216,10 +227,10 @@
     near = col // shard
     apart = near * shard + row - (col - near * shard)
     allowed = (apart >= 0) & (apart < ROW) & (near <= r)
-    columns = [None] * (4 * heads)
+    local_probs, lses, deltas = [], [], []
     for h in range(heads):
         kv.finish(h)
-        q, keys, values, do = qw[h, slot(0)], kvw[0, h], kvw[1, h], dow[h, slot(0)]
+        q, keys, values = qw[h, slot(0)], kvw[0, h], kvw[1, h]
         scores = jnp.where(allowed, dot_nt(q, keys) * scale, -jnp.inf)
         largest = jnp.max(scores, axis=1, keepdims=True)
         raised = jnp.exp(scores - largest)
@@ -227,13 +238,14 @@
         probs = raised / sums
         out = dot_nn(probs.astype(BF16), values).astype(BF16)
         att[:, h * width:(h + 1) * width] = out
-        delta = jnp.sum(do.astype(F32) * out.astype(F32), axis=1, keepdims=True)
-        columns[h], columns[heads + h] = largest + jnp.log(sums), delta
-        grad_s = (probs * (dot_nt(do, values) - delta)).astype(BF16)
-        grads[0, 0, h] = (dot_nn(grad_s, keys) * scale).astype(BF16)
-        if h == 0:
-            for e in steps[:-1]:
-                cotangent.pass_on(e)
+        lses.append(largest + jnp.log(sums))
+        deltas.append(delta_of(dow[h, slot(0)], out))
+        local_probs.append(probs)
+    near_stats[0] = as_rows(lses + deltas)
+    for d in range(1, back + 1):
+        pl.when(before(d))(lambda d=d: near_copy(d).start())
+    for e in steps[:-1]:
+        cotangent.pass_on(e)
 
     for j in far:
         pl.when(before(back * j))(lambda j=j: skv_copy(j).wait_recv())
@@ -244,9 +256,9 @@
     def value_of(j, h):
         return (qkv[1, 2, h] if j == 0 else skv[j - 1, 1, h]).astype(F32)
 
-    strided_probs = []
-    for h in range(heads):
-        q, do = qkv[1, 0, h].astype(F32), sdow[lines - 1, h].astype(F32)
+    strided_probs, strided_lses, strided_deltas = [], [], []
+    for h in range(heads):
+        q = qkv[1, 0, h].astype(F32)
         scores = [jnp.sum(q * key_of(0, h), axis=1, keepdims=True) * scale]
         for j in far:
             score = jnp.sum(q * key_of(j, h), axis=1, keepdims=True) * scale
@@ -259,27 +271,27 @@
         out = sum(p.astype(BF16).astype(F32) * value_of(j, h) for j, p in enumerate(probs))
         out = out.astype(BF16)
         att[:, (heads + h) * width:(heads + h + 1) * width] = out
-        columns[2 * heads + h] = largest + jnp.log(sums)
-        columns[3 * heads + h] = jnp.sum(do * out.astype(F32), axis=1, keepdims=True)
-
-    lane = lax.broadcasted_iota(jnp.int32, (shard, 128), 1)
-    table = jnp.zeros((shard, 128), F32)
-    for i, column in enumerate(columns):
-        table = jnp.where(lane == i, column, table)
-    stats[0] = table.T[:stats.shape[1]]
-    for i, d in enumerate(spans):
-        pl.when(before(d))(lambda i=i: stat_copy(i).start())
+        strided_lses.append(largest + jnp.log(sums))
+        strided_deltas.append(delta_of(sdow[lines - 1, h], out))
+    far_stats[0] = as_rows(strided_lses + strided_deltas)
+    for j in far:
+        pl.when(before(back * j))(lambda j=j: far_copy(j).start())
 
     for i, (to, _) in enumerate(partners):
         mxs[i] = dot_nn(att[...], w_cols(to)).astype(BF16)
         mx_copy(i).start()
     cotangent.pass_on(back)
+
+    for h in range(heads):
+        grad_p = dot_nt(dow[h, slot(0)], kvw[1, h])
+        grad_s = (local_probs[h] * (grad_p - deltas[h])).astype(BF16)
+        grads[0, 0, h] = (dot_nn(grad_s, kvw[0, h]) * scale).astype(BF16)
     total = dot_nn(att[...], w_cols(me))
 
     strided = []
     for h in range(heads):
         q, do = qkv[1, 0, h].astype(F32), sdow[lines - 1, h].astype(F32)
-        delta = columns[3 * heads + h]
+        delta = strided_deltas[h]
         grad_q = jnp.zeros_like(q)
         for j in [0] + far:
             prob = strided_probs[h][j]
@@ -290,18 +302,17 @@
                 strided.append((grad_s * q, prob.astype(BF16).astype(F32) * do))
         grads[1, 0, h] = (grad_q * scale).astype(BF16)
 
-    for i, d in enumerate(spans):
-        pl.when(after(d))(lambda i=i: stat_copy(i).wait_recv())
+    for d in range(1, back + 1):
+        pl.when(after(d))(lambda d=d: near_copy(d).wait_recv())
     apart = col - row
     allowed = (apart >= 0) & (apart < ROW) & (near < seq_count - r)
-    later = [0] + [spans.index(d) + 1 for d in range(1, back + 1) if d in spans]
-    later += [0] * (back + 1 - len(later))
     for h in range(heads):
         query.finish(h)
         cotangent.finish(h)
         queries, dos, key, value = qw[h], dow[h], kvw[0, h, slot(0)], kvw[1, h, slot(0)]
-        lse = jnp.concatenate([stats[i, h:h + 1] for i in later], axis=1)
-        delta = jnp.concatenate([stats[i, heads + h:heads + h + 1] for i in later], axis=1)
+        lse = jnp.concatenate([near_stats[d, h:h + 1] for d in range(back + 1)], axis=1)
+        rows = [near_stats[d, heads + h:heads + h + 1] for d in range(back + 1)]
+        delta = jnp.concatenate(rows, axis=1)
         probs = jnp.exp(jnp.where(allowed, dot_nt(key, queries) * scale - lse, -jnp.inf))
         grad_s = (probs * (dot_nt(value, dos) - delta)).astype(BF16)
         grads[0, 1, h] = (dot_nn(grad_s, queries) * scale).astype(BF16)
@@ -312,13 +323,14 @@
         def _(j=j):
             sq_copy(j).wait_recv()
             sdo_copy(j).wait_recv()
-    for j in far:
-        rows = stats[spans.index(back * j) + 1]
+            far_copy(j).wait_recv()
+    for j in far:
+        rows = far_stats[j]
         table = jnp.concatenate([rows] * (128 // rows.shape[0]), axis=0).T
         for h in range(heads):
             q, do = sqw[j - 1, h].astype(F32), sdow[j - 1, h].astype(F32)
-            lse = table[:, 2 * heads + h:2 * heads + h + 1]
-            delta = table[:, 3 * heads + h:3 * heads + h + 1]
+            lse = table[:, h:h + 1]
+            delta = table[:, heads + h:heads + h + 1]
             score = jnp.sum(q * key_of(0, h), axis=1, keepdims=True) * scale
             prob = jnp.exp(jnp.where(after(back * j), score - lse, -jnp.inf))
             grad_p = jnp.sum(do * value_of(0, h), axis=1, keepdims=True)
@@ -346,8 +358,9 @@
         def _(j=j):
             sq_copy(j).wait_send()
             sdo_copy(j).wait_send()
-    for i, d in enumerate(spans):
-        pl.when(before(d))(lambda i=i: stat_copy(i).wait_send())
+            far_copy(j).wait_send()
+    for d in range(1, back + 1):
+        pl.when(before(d))(lambda d=d: near_copy(d).wait_send())
 
 
 def shards(seq_count, head_groups, qkv, out_weight, out_grad):
@@ -357,15 +370,15 @@
     assert head_groups % 2 == 0
     lines = seq_count // back
     others = max(1, lines - 1)
-    spans = [d for d in range(1, back + 1) if d < seq_count]
+    spans = list(range(1, back + 1))
     spans += [back * j for j in range(2, lines)]
     model = out_weight.shape[-1]
     cols = out_grad.shape[1]
     window = (back + 1) * shard
-    stat_rows = 4 * heads
+    stat_rows = 2 * heads
     while 128 % stat_rows or stat_rows % 8:
         stat_rows += 1
-    copies = 2 * head_groups + 3 * lines + 3 * (back + 1) * heads + len(spans)
+    copies = 2 * head_groups + 3 * lines + 3 * (back + 1) * heads + back + 1 + lines
     vmem = pl.BlockSpec(memory_space=pltpu.VMEM)
     hbm = pl.BlockSpec(memory_space=pltpu.HBM)
     mixed, grads = pl.pallas_call(
@@ -390,13 +403,14 @@
             pltpu.VMEM((head_groups - 1, shard, cols), BF16),
             pltpu.VMEM((head_groups - 1, shard, cols), BF16),
             pltpu.VMEM((shard, 2 * heads * width), BF16),
-            pltpu.VMEM((len(spans) + 1, stat_rows, shard), F32),
+            pltpu.VMEM((back + 1, stat_rows, shard), F32),
+            pltpu.VMEM((lines, stat_rows, shard), F32),
             pltpu.SemaphoreType.DMA((5,)),
             pltpu.SemaphoreType.DMA((copies,)),
             pltpu.SemaphoreType.DMA((copies,)),
         ],
         compiler_params=pltpu.CompilerParams(
-            collective_id=0, has_side_effects=True, vmem_limit_bytes=40 * 1024 * 1024
+            collective_id=0, has_side_effects=True, vmem_limit_bytes=52 * 1024 * 1024
         ),
     )(
         jnp.swapaxes(qkv, 2, 3),

time: 33.7 us -> 30.7 us (0.911); the launches traced: 33.1 us -> 30.5 us
  local copies, waits for them, and re-layouts: 5.35 us -> 3.76 us
  Pallas kernels: 27.1 us -> 26.1 us
    unnamed x7 -> x5, local copies, waits for them, and re-layouts: 5.35 us -> 3.76 us
    pallas_call x1, Pallas kernels: 27.1 us -> 26.1 us  [shards(): pl.pallas_call(functools.partial(layer_kernel, seq_count, head_groups, ba...]
where the time goes in v2:
time: 30.7 us; the launch traced here: 30.5 us
  Pallas kernels  26.1 us (85%)
  local copies, waits for them, and re-layouts  3.76 us (12%)
  between operations  0.65 us (2%)
    pallas_call x1, Pallas kernels, shards(): pl.pallas_call(functools.partial(layer_kernel, seq_count, head_groups, ba...  26.1 us
    unnamed x5, local copies, waits for them, and re-layouts  3.76 us

profile of v2, /device:TPU:1, one launch (start us, length us, event | category | flops | bytes accessed | tf_op | source)
XLA Modules:
  0.0 30.5 jit_solution(1130373521854927549)
XLA Ops:
  0.6 1.1 %copy.8 = bf16[2,3,128,2,128]{4,2,3,1,0:T(8,128)(2,1)S(1)} copy(bf16[2,3,128,2,128]{4,3,2,1,0:T(2,128)(2,1)} %param.3) | data formatting | bytes 786432 | tf_op args[0]
  1.7 0.0 copy-start
  1.7 0.9 %copy-done = bf16[128,512]{1,0:T(8,128)(2,1)S(1)} copy-done((bf16[128,512]{1,0:T(8,128)(2,1)S(1)}, bf16[128,512]{1,0:T(8,128)(2,1)}, u32[]{:S(2)}) %copy-start) | copy-done | bytes 131096
  2.6 26.1 %shard_map.50 = (bf16[128,512]{1,0:T(8,128)(2,1)S(1)}, bf16[2,3,2,128,128]{4,3,2,1,0:T(8,128)(2,1)S(1)}) custom-call(bf16[2,3,2,128,128]{4,3,2,1,0:T(8,128)(2,1)S(1)} %bitcast.5, bf16[512,2048]{1,0:T(8,128)(2,1)} %bitcast.7, bf16[128,512]{1,0:T(8,128)(2,1)S(1)} %copy-done), custom_call_target="tpu_custom_call" | custom-call | tf_op jit(solution)/shard_map/pallas_call | solution.py:384
  28.7 1.2 %copy.6 = bf16[2,3,128,2,128]{4,3,2,1,0:T(2,128)(2,1)} copy(bf16[2,3,128,2,128]{4,2,3,1,0:T(8,128)(2,1)S(1)} %bitcast.6) | data formatting | bytes 786432
  29.9 0.7 %copy.10 = bf16[128,512]{1,0:T(8,128)(2,1)} copy(bf16[128,512]{1,0:T(8,128)(2,1)S(1)} %get-tuple-element.10) | data formatting | bytes 262144
Async XLA Ops:
  1.7 0.9 %copy-start = (bf16[128,512]{1,0:T(8,128)(2,1)S(1)}, bf16[128,512]{1,0:T(8,128)(2,1)}, u32[]{:S(2)}) copy-start(bf16[128,512]{1,0:T(8,128)(2,1)} %og_hbm.1) | copy-start | bytes 393220

commit v3 on v2

--- a/solution.py
+++ b/solution.py
@@ -158,11 +158,16 @@
     skv_at, sq_at, sdo_at = numbered(lines), numbered(lines), numbered(lines)
     near_at, far_at = numbered(back + 1), numbered(lines)
 
+    last = len(partners) - 1
+
+    def group_of(i):
+        return {"head": partners[last if i % 2 else i][0]}
+
     def og_copy(i):
-        return remote(og, ogf.at[i], og_at + i, {"head": partners[i][0]})
+        return remote(ogf.at[i - 1] if i % 2 else og, ogf.at[i], og_at + i, group_of(i))
 
     def mx_copy(i):
-        return remote(mxs.at[i], mxr.at[i], mx_at + i, {"head": partners[i][0]})
+        return remote(mxs.at[i], mxr.at[i], mx_at + i, group_of(i))
 
     def skv_copy(j):
         return remote(qkv.at[1, 1:3], skv.at[j - 1], skv_at + j, {"seq": r + back * j})
@@ -193,7 +198,7 @@
         load.wait()
     pl.semaphore_wait(barrier, expected)
     kv.pass_on(0)
-    for i in range(len(partners)):
+    for i in range(0, last + 1, 2):
         og_copy(i).start()
     query.pass_on(0)
     for load in loads[3:]:
@@ -202,15 +207,22 @@
     def w_cols(group):
         return w[:, pl.ds(pl.multiple_of(group * cols, cols), cols)]
 
-    total = dot_nt(og[...], w_cols(me))
     for e in steps:
         kv.pass_on(e)
         query.pass_on(e)
+        if e == steps[0]:
+            for i in range(0, last, 2):
+                og_copy(i).wait_recv()
+                og_copy(i + 1).start()
+            og_copy(last).wait_recv()
+            total = dot_nt(og[...], w_cols(me))
+            for i in range(0, last + 1, 2):
+                total += dot_nt(ogf[i], w_cols(partners[i][1]))
     for j in far:
         pl.when(after(back * j))(lambda j=j: skv_copy(j).start())
         pl.when(before(back * j))(lambda j=j: sq_copy(j).start())
 
-    for i in reversed(range(len(partners))):
+    for i in range(1, last, 2):
         og_copy(i).wait_recv()
         total += dot_nt(ogf[i], w_cols(partners[i][1]))
     total = total.astype(BF16)
@@ -241,11 +253,12 @@
         lses.append(largest + jnp.log(sums))
         deltas.append(delta_of(dow[h, slot(0)], out))
         local_probs.append(probs)
+        if h == 0:
+            for e in steps[:-1]:
+                cotangent.pass_on(e)
     near_stats[0] = as_rows(lses + deltas)
     for d in range(1, back + 1):
         pl.when(before(d))(lambda d=d: near_copy(d).start())
-    for e in steps[:-1]:
-        cotangent.pass_on(e)
 
     for j in far:
         pl.when(before(back * j))(lambda j=j: skv_copy(j).wait_recv())
@@ -277,9 +290,16 @@
     for j in far:
         pl.when(before(back * j))(lambda j=j: far_copy(j).start())
 
-    for i, (to, _) in enumerate(partners):
-        mxs[i] = dot_nn(att[...], w_cols(to)).astype(BF16)
+    for i in range(1, last, 2):
+        mxs[i] = dot_nn(att[...], w_cols(partners[i][0])).astype(BF16)
         mx_copy(i).start()
+    for i in range(0, last, 2):
+        total = dot_nn(att[...], w_cols(partners[i][0]))
+        mx_copy(i + 1).wait_recv()
+        mxs[i] = (total + mxr[i + 1].astype(F32)).astype(BF16)
+        mx_copy(i).start()
+    mxs[last] = dot_nn(att[...], w_cols(partners[last][0])).astype(BF16)
+    mx_copy(last).start()
     cotangent.pass_on(back)
 
     for h in range(heads):
@@ -341,7 +361,7 @@
         grads[1, 1, h] = (strided[h][0] * scale).astype(BF16)
         grads[1, 2, h] = strided[h][1].astype(BF16)
 
-    for i in reversed(range(len(partners))):
+    for i in range(last, -1, -2):
         mx_copy(i).wait_recv()
         total += mxr[i].astype(F32)
     mixed[...] = total.astype(BF16)

time: 30.7 us -> 31.6 us (1.029)
  Pallas kernels: 26.1 us -> 26.9 us
    pallas_call x1, Pallas kernels: 26.1 us -> 26.9 us  [shards(): pl.pallas_call(functools.partial(layer_kernel, seq_count, head_groups, ba...]
where the time goes in v3:
time: 31.6 us; the launch traced here: 31.3 us
  Pallas kernels  26.9 us (85%)
  local copies, waits for them, and re-layouts  3.76 us (12%)
  between operations  0.65 us (2%)
    pallas_call x1, Pallas kernels, shards(): pl.pallas_call(functools.partial(layer_kernel, seq_count, head_groups, ba...  26.9 us
    unnamed x5, local copies, waits for them, and re-layouts  3.76 us

profile of v3, /device:TPU:1, one launch (start us, length us, event | category | flops | bytes accessed | tf_op | source)
XLA Modules:
  0.0 31.3 jit_solution(2262207205182822978)
XLA Ops:
  0.6 1.1 %copy.8 = bf16[2,3,128,2,128]{4,2,3,1,0:T(8,128)(2,1)S(1)} copy(bf16[2,3,128,2,128]{4,3,2,1,0:T(2,128)(2,1)} %param.3) | data formatting | bytes 786432 | tf_op args[0]
  1.7 0.0 copy-start
  1.7 0.9 %copy-done = bf16[128,512]{1,0:T(8,128)(2,1)S(1)} copy-done((bf16[128,512]{1,0:T(8,128)(2,1)S(1)}, bf16[128,512]{1,0:T(8,128)(2,1)}, u32[]{:S(2)}) %copy-start) | copy-done | bytes 131096
  2.6 26.9 %shard_map.50 = (bf16[128,512]{1,0:T(8,128)(2,1)S(1)}, bf16[2,3,2,128,128]{4,3,2,1,0:T(8,128)(2,1)S(1)}) custom-call(bf16[2,3,2,128,128]{4,3,2,1,0:T(8,128)(2,1)S(1)} %bitcast.5, bf16[512,2048]{1,0:T(8,128)(2,1)} %bitcast.7, bf16[128,512]{1,0:T(8,128)(2,1)S(1)} %copy-done), custom_call_target="tpu_custom_call" | custom-call | tf_op jit(solution)/shard_map/pallas_call | solution.py:404
  29.5 1.2 %copy.6 = bf16[2,3,128,2,128]{4,3,2,1,0:T(2,128)(2,1)} copy(bf16[2,3,128,2,128]{4,2,3,1,0:T(8,128)(2,1)S(1)} %bitcast.6) | data formatting | bytes 786432
  30.7 0.7 %copy.10 = bf16[128,512]{1,0:T(8,128)(2,1)} copy(bf16[128,512]{1,0:T(8,128)(2,1)S(1)} %get-tuple-element.10) | data formatting | bytes 262144
Async XLA Ops:
  1.7 0.9 %copy-start = (bf16[128,512]{1,0:T(8,128)(2,1)S(1)}, bf16[128,512]{1,0:T(8,128)(2,1)}, u32[]{:S(2)}) copy-start(bf16[128,512]{1,0:T(8,128)(2,1)} %og_hbm.1) | copy-start | bytes 393220

commit v4 on v2

--- a/solution.py
+++ b/solution.py
@@ -156,7 +156,7 @@
     cotangent = Cascade(-1, lambda h, rows: dow.at[h, rows])
     og_at, mx_at = numbered(head_groups), numbered(head_groups)
     skv_at, sq_at, sdo_at = numbered(lines), numbered(lines), numbered(lines)
-    near_at, far_at = numbered(back + 1), numbered(lines)
+    near_at, far_at = numbered((back + 1) * heads), numbered(lines)
 
     def og_copy(i):
         return remote(og, ogf.at[i], og_at + i, {"head": partners[i][0]})
@@ -173,8 +173,9 @@
     def sdo_copy(j):
         return remote(sdow.at[lines - 1], sdow.at[j - 1], sdo_at + j, {"seq": r - back * j})
 
-    def near_copy(d):
-        return remote(near_stats.at[0], near_stats.at[d], near_at + d, {"seq": r - d})
+    def near_copy(d, h):
+        at = near_at + d * heads + h
+        return remote(near_stats.at[0, h], near_stats.at[d, h], at, {"seq": r - d})
 
     def far_copy(j):
         return remote(far_stats.at[0], far_stats.at[j], far_at + j, {"seq": r - back * j})
@@ -184,7 +185,7 @@
         table = jnp.zeros((shard, 128), F32)
         for i, column in enumerate(columns):
             table = jnp.where(lane == i, column, table)
-        return table.T[:near_stats.shape[1]]
+        return table.T[:far_stats.shape[1]]
 
     def delta_of(do, out):
         return jnp.sum(do.astype(F32) * out.astype(F32), axis=1, keepdims=True)
@@ -218,8 +219,6 @@
         dow[h, slot(0)] = total[:, h * width:(h + 1) * width]
         sdow[lines - 1, h] = total[:, (heads + h) * width:(heads + h + 1) * width]
     cotangent.pass_on(0)
-    for j in far:
-        pl.when(before(back * j))(lambda j=j: sdo_copy(j).start())
 
     window = (back + 1) * shard
     row = lax.broadcasted_iota(jnp.int32, (shard, window), 0)
@@ -227,7 +226,7 @@
     near = col // shard
     apart = near * shard + row - (col - near * shard)
     allowed = (apart >= 0) & (apart < ROW) & (near <= r)
-    local_probs, lses, deltas = [], [], []
+    local_probs, deltas = [], []
     for h in range(heads):
         kv.finish(h)
         q, keys, values = qw[h, slot(0)], kvw[0, h], kvw[1, h]
@@ -238,14 +237,16 @@
         probs = raised / sums
         out = dot_nn(probs.astype(BF16), values).astype(BF16)
         att[:, h * width:(h + 1) * width] = out
-        lses.append(largest + jnp.log(sums))
         deltas.append(delta_of(dow[h, slot(0)], out))
         local_probs.append(probs)
-    near_stats[0] = as_rows(lses + deltas)
-    for d in range(1, back + 1):
-        pl.when(before(d))(lambda d=d: near_copy(d).start())
-    for e in steps[:-1]:
-        cotangent.pass_on(e)
+        near_stats[0, h] = as_rows([largest + jnp.log(sums), deltas[h]])
+        for d in range(1, back + 1):
+            pl.when(before(d))(lambda d=d, h=h: near_copy(d, h).start())
+        if h == 0:
+            for e in steps[:-1]:
+                cotangent.pass_on(e)
+            for j in far:
+                pl.when(before(back * j))(lambda j=j: sdo_copy(j).start())
 
     for j in far:
         pl.when(before(back * j))(lambda j=j: skv_copy(j).wait_recv())
@@ -302,16 +303,16 @@
                 strided.append((grad_s * q, prob.astype(BF16).astype(F32) * do))
         grads[1, 0, h] = (grad_q * scale).astype(BF16)
 
-    for d in range(1, back + 1):
-        pl.when(after(d))(lambda d=d: near_copy(d).wait_recv())
     apart = col - row
     allowed = (apart >= 0) & (apart < ROW) & (near < seq_count - r)
     for h in range(heads):
         query.finish(h)
         cotangent.finish(h)
+        for d in range(1, back + 1):
+            pl.when(after(d))(lambda d=d, h=h: near_copy(d, h).wait_recv())
         queries, dos, key, value = qw[h], dow[h], kvw[0, h, slot(0)], kvw[1, h, slot(0)]
-        lse = jnp.concatenate([near_stats[d, h:h + 1] for d in range(back + 1)], axis=1)
-        rows = [near_stats[d, heads + h:heads + h + 1] for d in range(back + 1)]
+        lse = jnp.concatenate([near_stats[d, h, 0:1] for d in range(back + 1)], axis=1)
+        rows = [near_stats[d, h, 1:2] for d in range(back + 1)]
         delta = jnp.concatenate(rows, axis=1)
         probs = jnp.exp(jnp.where(allowed, dot_nt(key, queries) * scale - lse, -jnp.inf))
         grad_s = (probs * (dot_nt(value, dos) - delta)).astype(BF16)
@@ -360,7 +361,8 @@
             sdo_copy(j).wait_send()
             far_copy(j).wait_send()
     for d in range(1, back + 1):
-        pl.when(before(d))(lambda d=d: near_copy(d).wait_send())
+        for h in range(heads):
+            pl.when(before(d))(lambda d=d, h=h: near_copy(d, h).wait_send())
 
 
 def shards(seq_count, head_groups, qkv, out_weight, out_grad):
@@ -378,7 +380,7 @@
     stat_rows = 2 * heads
     while 128 % stat_rows or stat_rows % 8:
         stat_rows += 1
-    copies = 2 * head_groups + 3 * lines + 3 * (back + 1) * heads + back + 1 + lines
+    copies = 2 * head_groups + 3 * lines + 4 * (back + 1) * heads + lines
     vmem = pl.BlockSpec(memory_space=pltpu.VMEM)
     hbm = pl.BlockSpec(memory_space=pltpu.HBM)
     mixed, grads = pl.pallas_call(
@@ -403,7 +405,7 @@
             pltpu.VMEM((head_groups - 1, shard, cols), BF16),
             pltpu.VMEM((head_groups - 1, shard, cols), BF16),
             pltpu.VMEM((shard, 2 * heads * width), BF16),
-            pltpu.VMEM((back + 1, stat_rows, shard), F32),
+            pltpu.VMEM((back + 1, heads, stat_rows, shard), F32),
             pltpu.VMEM((lines, stat_rows, shard), F32),
             pltpu.SemaphoreType.DMA((5,)),
             pltpu.SemaphoreType.DMA((copies,)),

time: 30.7 us -> 31.5 us (1.026)
  Pallas kernels: 26.1 us -> 26.8 us
    pallas_call x1, Pallas kernels: 26.1 us -> 26.8 us  [shards(): pl.pallas_call(functools.partial(layer_kernel, seq_count, head_groups, ba...]
where the time goes in v4:
time: 31.5 us; the launch traced here: 31.3 us
  Pallas kernels  26.8 us (85%)
  local copies, waits for them, and re-layouts  3.76 us (12%)
  between operations  0.65 us (2%)
    pallas_call x1, Pallas kernels, shards(): pl.pallas_call(functools.partial(layer_kernel, seq_count, head_groups, ba...  26.8 us
    unnamed x5, local copies, waits for them, and re-layouts  3.76 us

profile of v4, /device:TPU:1, one launch (start us, length us, event | category | flops | bytes accessed | tf_op | source)
XLA Modules:
  0.0 31.3 jit_solution(9563905227380314752)
XLA Ops:
  0.6 1.1 %copy.8 = bf16[2,3,128,2,128]{4,2,3,1,0:T(8,128)(2,1)S(1)} copy(bf16[2,3,128,2,128]{4,3,2,1,0:T(2,128)(2,1)} %param.3) | data formatting | bytes 786432 | tf_op args[0]
  1.7 0.0 copy-start
  1.7 0.9 %copy-done = bf16[128,512]{1,0:T(8,128)(2,1)S(1)} copy-done((bf16[128,512]{1,0:T(8,128)(2,1)S(1)}, bf16[128,512]{1,0:T(8,128)(2,1)}, u32[]{:S(2)}) %copy-start) | copy-done | bytes 131096
  2.6 26.8 %shard_map.50 = (bf16[128,512]{1,0:T(8,128)(2,1)S(1)}, bf16[2,3,2,128,128]{4,3,2,1,0:T(8,128)(2,1)S(1)}) custom-call(bf16[2,3,2,128,128]{4,3,2,1,0:T(8,128)(2,1)S(1)} %bitcast.5, bf16[512,2048]{1,0:T(8,128)(2,1)} %bitcast.7, bf16[128,512]{1,0:T(8,128)(2,1)S(1)} %copy-done), custom_call_target="tpu_custom_call" | custom-call | tf_op jit(solution)/shard_map/pallas_call | solution.py:386
  29.4 1.2 %copy.6 = bf16[2,3,128,2,128]{4,3,2,1,0:T(2,128)(2,1)} copy(bf16[2,3,128,2,128]{4,2,3,1,0:T(8,128)(2,1)S(1)} %bitcast.6) | data formatting | bytes 786432
  30.6 0.7 %copy.10 = bf16[128,512]{1,0:T(8,128)(2,1)} copy(bf16[128,512]{1,0:T(8,128)(2,1)S(1)} %get-tuple-element.10) | data formatting | bytes 262144
Async XLA Ops:
  1.7 0.9 %copy-start = (bf16[128,512]{1,0:T(8,128)(2,1)S(1)}, bf16[128,512]{1,0:T(8,128)(2,1)}, u32[]{:S(2)}) copy-start(bf16[128,512]{1,0:T(8,128)(2,1)} %og_hbm.1) | copy-start | bytes 393220

commit v5 on v2

--- a/solution.py
+++ b/solution.py
@@ -221,12 +221,16 @@
     for j in far:
         pl.when(before(back * j))(lambda j=j: sdo_copy(j).start())
 
-    window = (back + 1) * shard
-    row = lax.broadcasted_iota(jnp.int32, (shard, window), 0)
-    col = lax.broadcasted_iota(jnp.int32, (shard, window), 1)
-    near = col // shard
-    apart = near * shard + row - (col - near * shard)
-    allowed = (apart >= 0) & (apart < ROW) & (near <= r)
+    ahead = lax.broadcasted_iota(jnp.int32, (shard, shard), 0) - lax.broadcasted_iota(
+        jnp.int32, (shard, shard), 1
+    )
+
+    def band(ahead, there):
+        blocks = [d * shard + ahead for d in range(back + 1)]
+        blocks = [(a >= 0) & (a < ROW) & there(d) for d, a in enumerate(blocks)]
+        return jnp.concatenate(blocks, axis=1)
+
+    allowed = band(ahead, before)
     local_probs, lses, deltas = [], [], []
     for h in range(heads):
         kv.finish(h)
@@ -235,7 +239,7 @@
         largest = jnp.max(scores, axis=1, keepdims=True)
         raised = jnp.exp(scores - largest)
         sums = jnp.sum(raised, axis=1, keepdims=True)
-        probs = raised / sums
+        probs = raised * (1.0 / sums)
         out = dot_nn(probs.astype(BF16), values).astype(BF16)
         att[:, h * width:(h + 1) * width] = out
         lses.append(largest + jnp.log(sums))
@@ -304,8 +308,7 @@
 
     for d in range(1, back + 1):
         pl.when(after(d))(lambda d=d: near_copy(d).wait_recv())
-    apart = col - row
-    allowed = (apart >= 0) & (apart < ROW) & (near < seq_count - r)
+    allowed = band(-ahead, after)
     for h in range(heads):
         query.finish(h)
         cotangent.finish(h)

time: 30.7 us -> 30.7 us (level)
  no operation moved by 1% of the time
where the time goes in v5:
time: 30.7 us; the launch traced here: 30.6 us
  Pallas kernels  26.1 us (85%)
  local copies, waits for them, and re-layouts  3.76 us (12%)
  between operations  0.65 us (2%)
    pallas_call x1, Pallas kernels, shards(): pl.pallas_call(functools.partial(layer_kernel, seq_count, head_groups, ba...  26.1 us
    unnamed x5, local copies, waits for them, and re-layouts  3.76 us

profile of v5, /device:TPU:1, one launch (start us, length us, event | category | flops | bytes accessed | tf_op | source)
XLA Modules:
  0.0 30.6 jit_solution(17801738288719756493)
XLA Ops:
  0.6 1.1 %copy.8 = bf16[2,3,128,2,128]{4,2,3,1,0:T(8,128)(2,1)S(1)} copy(bf16[2,3,128,2,128]{4,3,2,1,0:T(2,128)(2,1)} %param.3) | data formatting | bytes 786432 | tf_op args[0]
  1.7 0.0 copy-start
  1.7 0.9 %copy-done = bf16[128,512]{1,0:T(8,128)(2,1)S(1)} copy-done((bf16[128,512]{1,0:T(8,128)(2,1)S(1)}, bf16[128,512]{1,0:T(8,128)(2,1)}, u32[]{:S(2)}) %copy-start) | copy-done | bytes 131096
  2.6 26.1 %shard_map.50 = (bf16[128,512]{1,0:T(8,128)(2,1)S(1)}, bf16[2,3,2,128,128]{4,3,2,1,0:T(8,128)(2,1)S(1)}) custom-call(bf16[2,3,2,128,128]{4,3,2,1,0:T(8,128)(2,1)S(1)} %bitcast.5, bf16[512,2048]{1,0:T(8,128)(2,1)} %bitcast.7, bf16[128,512]{1,0:T(8,128)(2,1)S(1)} %copy-done), custom_call_target="tpu_custom_call" | custom-call | tf_op jit(solution)/shard_map/pallas_call | solution.py:387
  28.7 1.2 %copy.6 = bf16[2,3,128,2,128]{4,3,2,1,0:T(2,128)(2,1)} copy(bf16[2,3,128,2,128]{4,2,3,1,0:T(8,128)(2,1)S(1)} %bitcast.6) | data formatting | bytes 786432
  29.9 0.7 %copy.10 = bf16[128,512]{1,0:T(8,128)(2,1)} copy(bf16[128,512]{1,0:T(8,128)(2,1)S(1)} %get-tuple-element.10) | data formatting | bytes 262144
Async XLA Ops:
  1.7 0.9 %copy-start = (bf16[128,512]{1,0:T(8,128)(2,1)S(1)}, bf16[128,512]{1,0:T(8,128)(2,1)}, u32[]{:S(2)}) copy-start(bf16[128,512]{1,0:T(8,128)(2,1)} %og_hbm.1) | copy-start | bytes 393220
